TPU v7x, 32 devices: a whole 2x2x4 slice. The times are simulated.
32 devices in a mesh: row: 4 (over y, x), seq: 8 (over z, core).
Axes of the slice: x: 2, y: 2, z: 4, core: 2. Of those that a mesh axis runs over, the one named last changes fastest.
Arguments:
- signal: bfloat16 [4, 16384, 512], P('row', 'seq'), may hold values from -6 to 6
- condition: bfloat16 [4, 16384, 80], P('row', 'seq'), may hold values from -6 to 6
- lengths: int32 [4, 4], P('row'), may hold values from 1 to 15360, 16384 in all within a row
- owner: int32 [256], replicated, may hold values from 0 to 255, each once
- grad_out: bfloat16 [4, 16384, 512], P('row', 'seq'), may hold values from -6 to 6
- grad_skip: bfloat16 [4, 16384, 512], P('row', 'seq'), may hold values from -6 to 6
- w_in: float32 [256, 69, 128], P(('row', 'seq')), may hold values from -0.1875 to 0.1875
- w_out: float32 [256, 64, 64], P(('row', 'seq')), may hold values from -0.75 to 0.75
- left_in: float32 [256, 69, 69], P(('row', 'seq')), as said below
- right_in: float32 [256, 128, 128], P(('row', 'seq')), as said below
- root_left_in: float32 [256, 69, 69], P(('row', 'seq')), as said below
- root_right_in: float32 [256, 128, 128], P(('row', 'seq')), as said below
- left_out: float32 [256, 64, 64], P(('row', 'seq')), as said below
- right_out: float32 [256, 64, 64], P(('row', 'seq')), as said below
- root_left_out: float32 [256, 64, 64], P(('row', 'seq')), as said below
- root_right_out: float32 [256, 64, 64], P(('row', 'seq')), as said below
Outputs:
- out_x: float32 [4, 16384, 512], P('row', 'seq')
- skip_sum: float32 [4, 16384, 512], P('row', 'seq')
- grad_x: float32 [4, 16384, 512], P('row', 'seq')
- grad_cond: float32 [4, 16384, 80], P('row', 'seq')
- grad_in_blocks: float32 [256, 69, 128], P(('row', 'seq'))
- grad_out_blocks: float32 [256, 64, 64], P(('row', 'seq'))
- new_left_in: float32 [256, 69, 69], P(('row', 'seq'))
- new_right_in: float32 [256, 128, 128], P(('row', 'seq'))
- new_left_out: float32 [256, 64, 64], P(('row', 'seq'))
- new_right_out: float32 [256, 64, 64], P(('row', 'seq'))
- new_w_in: float32 [256, 69, 128], P(('row', 'seq'))
- new_w_out: float32 [256, 64, 64], P(('row', 'seq'))
Inputs may be any that keep to these rules, and one draw needn't show every extreme that they name: `lengths`: each packed row is filled exactly; its longest utterance has exactly 15360 samples. `owner`: a permutation of the block numbers. `left_in`: symmetric matrices. `right_in`: symmetric matrices. `root_left_in`: symmetric matrices. `root_right_in`: symmetric matrices. `left_out`: symmetric matrices. `right_out`: symmetric matrices. `root_left_out`: symmetric matrices. `root_right_out`: symmetric matrices.
All inputs are finite; a program needn't handle non-finite values.
Results may differ from a plain program's by a relative error of at most 0.0086.
Values may be sent and summed in bfloat16 or wider, within the bound.
A program may use at most 256 MiB of HBM per device.

v0:
```python
import jax
import jax.numpy as jnp
from jax import lax
from jax.experimental import pallas as pl
from jax.experimental.pallas import tpu as pltpu
from jax.sharding import PartitionSpec as P

FIRST_DILATION = 512
MESH = pl.DeviceIdType.MESH
bf16, f32, i32 = jnp.bfloat16, jnp.float32, jnp.int32

highest = lax.Precision.HIGHEST
rate_in = 0.3
rate_out = 1.0

TILE = 512
ROWS_IN = 576
ROWS_OUT = 256


def shifted(block, axis, distance):
    devices = range(lax.axis_size(axis))
    route = [(i - distance, i) for i in devices if i - distance in devices]
    return lax.ppermute(block, axis, route)


def to_blocks(full, row_parts, col_parts):
    layers, rows, cols = full.shape
    shaped = full.reshape(layers, row_parts, rows // row_parts, col_parts, cols // col_parts)
    return shaped.transpose(0, 1, 3, 2, 4).reshape(
        layers * row_parts * col_parts, rows // row_parts, cols // col_parts
    )


def from_blocks(blocks, row_parts, col_parts):
    count, block_rows, block_cols = blocks.shape
    layers = count // (row_parts * col_parts)
    shaped = blocks.reshape(layers, row_parts, col_parts, block_rows, block_cols)
    return shaped.transpose(0, 1, 3, 2, 4).reshape(
        layers, row_parts * block_rows, col_parts * block_cols
    )


def receptive_mask(lengths, sample_positions, dilation):
    ends = jnp.cumsum(lengths, axis=1)
    starts = jnp.sum(
        jnp.where(ends[:, None, :] <= sample_positions[None, :, None], lengths[:, None, :], 0),
        axis=2,
    )
    return sample_positions[None, :] - dilation >= starts


def gate_forward(units, input_weight, output_weight):
    pre = jnp.einsum("ptk,kg->ptg", units, input_weight, preferred_element_type=jnp.float32)
    half = pre.shape[2] // 2
    tanh_part = jnp.tanh(pre[..., :half])
    sigm_part = jax.nn.sigmoid(pre[..., half:])
    hidden = (tanh_part * sigm_part).astype(jnp.bfloat16)
    projected = jnp.einsum("ptg,gk->ptk", hidden, output_weight, preferred_element_type=jnp.float32)
    return (tanh_part, sigm_part, hidden, projected)


def gate_backward(
    units, tanh_part, sigm_part, hidden, input_weight, output_weight, grad_state, grad_skip
):
    grad_proj = jnp.concatenate([grad_state, grad_skip.astype(jnp.float32)], axis=2).astype(
        jnp.bfloat16
    )
    grad_wout = jnp.einsum("ptg,ptk->gk", hidden, grad_proj, preferred_element_type=jnp.float32)
    grad_hidden = jnp.einsum(
        "ptk,gk->ptg", grad_proj, output_weight, preferred_element_type=jnp.float32
    )
    grad_tanh = grad_hidden * sigm_part * (1.0 - tanh_part * tanh_part)
    grad_sigm = grad_hidden * tanh_part * sigm_part * (1.0 - sigm_part)
    grad_pre = jnp.concatenate([grad_tanh, grad_sigm], axis=2).astype(jnp.bfloat16)
    grad_win = jnp.einsum("ptk,ptg->kg", units, grad_pre, preferred_element_type=jnp.float32)
    grad_units = jnp.einsum(
        "ptg,kg->ptk", grad_pre, input_weight, preferred_element_type=jnp.float32
    )
    return (grad_win, grad_wout, grad_units)


def shampoo(grad, left, right, root_left, root_right, weight, rate):
    new_left = 0.5 * left + 0.5 * jnp.einsum("bij,bkj->bik", grad, grad, precision=highest)
    new_right = 0.5 * right + 0.5 * jnp.einsum("bji,bjk->bik", grad, grad, precision=highest)
    step = jnp.einsum("bij,bjk->bik", root_left, grad, precision=highest)
    step = jnp.einsum("bij,bjk->bik", step, root_right, precision=highest)
    return (new_left, new_right, weight - rate * step)


class Place:
    def __init__(self):
        self.row, self.seq = lax.axis_index("row"), lax.axis_index("seq")
        self.z, self.core = self.seq // 2, self.seq % 2
        x, y = self.row % 2, self.row // 2
        self.rows = (
            self.row,
            self.row + 1 - 2 * x,
            self.row + 2 - 4 * y,
            self.row + 3 - 2 * x - 4 * y,
        )
        self.x_peer = (self.rows[1], self.seq)
        self.y_peer = (self.rows[2], self.seq)
        self.sibling = (self.row, self.seq + 1 - 2 * self.core)
        self.near = self.mirrored(self.z)
        self.others = [self.mirrored(t) for t in (1 - self.near, 2, 3)]

    def mirrored(self, z):
        return z + self.z // 2 * (3 - 2 * z)

    def z_peer(self, z):
        return (self.row, 2 * z + self.core)

    def owner(self, rel, z, core=None):
        core = self.core if core is None else core
        return self.rows[rel] * 8 + 2 * z + core

    def announce(self):
        peers = [self.x_peer, self.y_peer, self.sibling] + [self.z_peer(z) for z in self.others]
        for peer in peers:
            pl.semaphore_signal(
                pltpu.get_barrier_semaphore(), inc=1, device_id=peer, device_id_type=MESH
            )

    def all_here(self):
        pl.semaphore_wait(pltpu.get_barrier_semaphore(), 6)


class Gather:
    def __init__(self, place, stack, count, sems):
        self.p, self.stack, self.count = place, stack, count
        self.send_sem, self.z_sems, self.x_sems, self.y_sems, self.s_sem = sems
        self.sent = 0

    def at(self, rel, z, half=None, core=None):
        start = self.p.owner(rel, z, core) * self.count
        if half is None:
            return self.stack.at[pl.ds(start, self.count)]
        part = self.count // 2
        return self.stack.at[pl.ds(start + half * part, part)]

    def copy(self, ref, sem, peer):
        return pltpu.make_async_remote_copy(
            src_ref=ref, dst_ref=ref, send_sem=self.send_sem.at[0], recv_sem=sem, device_id=peer, device_id_type=MESH
        )

    def send(self, ref, sem, peer):
        self.copy(ref, sem, peer).start()
        self.sent += 1

    def arrived(self, ref, sem, peer):
        self.copy(ref, sem, peer).wait_recv()

    def to_x(self, kind, rel, z, half):
        self.send(self.at(rel, z, half), self.x_sems.at[kind * 4 + z], self.p.x_peer)

    def to_y(self, kind, rel, z, half):
        self.send(self.at(rel, z, half), self.y_sems.at[kind * 4 + z], self.p.y_peer)

    def to_sibling(self, rel, z, half):
        self.send(self.at(rel, z, half), self.s_sem.at[0], self.p.sibling)

    def sides(self, z, half):
        if half == 0:
            self.to_x(0, 0, z, 0)
            self.to_y(1, 0, z, 0)
        else:
            self.to_y(0, 0, z, 1)
            self.to_x(1, 0, z, 1)
        self.to_sibling(0, z, half)

    def z_copy(self, src, half, z):
        return self.copy(self.at(0, src, half), self.z_sems.at[2 * src + half], self.p.z_peer(z))

    def z_passed(self, n, half):
        p = self.p
        outer, inner = p.mirrored(0), p.mirrored(2)
        near, far, farthest = p.others
        src, z = ((p.z, inner), (near, inner), (far, outer), (farthest, outer))[n]
        return self.z_copy(src, half, z)

    def pass_on(self, n, half):
        pl.when(self.p.near == 1)(lambda: self.z_passed(n, half).start())

    def start(self):
        p = self.p
        for half in range(2):
            self.z_copy(p.z, half, p.mirrored(1 - p.near)).start()
            self.sent += 1
            self.pass_on(0, half)

    def start_sides(self):
        for half in range(2):
            self.sides(self.p.z, half)

    def relay(self, n, half):
        z = self.p.others[n]
        self.arrived(self.at(0, z, half), self.z_sems.at[2 * z + half], self.p.z_peer(z))
        self.pass_on(n + 1, half)

    def spread(self, n, half):
        self.sides(self.p.others[n], half)

    def along_z(self, n):
        for half in range(2):
            self.relay(n, half)
            self.spread(n, half)

    def first(self, z):
        p = self.p
        self.arrived(self.at(1, z, 0), self.x_sems.at[z], p.x_peer)
        self.to_y(2, 1, z, 0)
        self.to_sibling(1, z, 0)
        self.arrived(self.at(2, z, 1), self.y_sems.at[z], p.y_peer)
        self.to_x(2, 2, z, 1)
        self.to_sibling(2, z, 1)

    def second(self, z):
        p = self.p
        self.arrived(self.at(1, z, 1), self.x_sems.at[4 + z], p.x_peer)
        self.to_sibling(1, z, 1)
        self.arrived(self.at(2, z, 0), self.y_sems.at[4 + z], p.y_peer)
        self.to_sibling(2, z, 0)

    def third(self, z):
        p = self.p
        self.arrived(self.at(3, z, 1), self.x_sems.at[8 + z], p.x_peer)
        self.to_sibling(3, z, 1)
        self.arrived(self.at(3, z, 0), self.y_sems.at[8 + z], p.y_peer)
        self.to_sibling(3, z, 0)

    def rest(self, z):
        self.second(z)
        self.third(z)

    def bytes_of(self, halves):
        return self.stack.at[pl.ds(0, halves * self.count // 2)]

    def finish(self):
        self.arrived(self.bytes_of(32), self.s_sem.at[0], self.p.sibling)
        self.copy(self.bytes_of(self.sent), self.s_sem.at[0], self.p.sibling).wait_send()

        @pl.when(self.p.near == 1)
        def _():
            self.copy(self.bytes_of(8), self.s_sem.at[0], self.p.sibling).wait_send()


GATHER_SEMS = [pltpu.SemaphoreType.DMA((n,)) for n in (1, 8, 12, 12, 1)]


def pick(which, zero, one):
    return jnp.where(jnp.full(zero.shape, which, i32) == 0, zero, one)


def assemble_in(inverse, stack, spread, weight, layer):
    def column(j, _):
        for i in range(16):
            q = inverse[layer, i * 8 + j]
            pair = stack[lax.div(q, 2)].astype(f32)
            spread[j, pl.ds(69 * i, 72), :] = pick(lax.rem(q, 2), pair[:72], pair[72:])
        weight[layer, :1104, pl.ds(pl.multiple_of(j * 128, 128), 128)] = spread[j, :1104, :].astype(bf16)
        return 0

    lax.fori_loop(0, 8, column, 0)


def across(top, bottom):
    left = lax.broadcasted_iota(i32, top.shape, 1) < 64
    return (
        jnp.where(left, top, pltpu.roll(bottom, 64, 1)),
        jnp.where(left, pltpu.roll(top, 64, 1), bottom),
    )


def assemble_out(inverse, stack, weight, layer):
    def line(i, _):
        for m in range(8):
            two = [stack[inverse[layer, i * 16 + 2 * m + h]].astype(f32) for h in range(2)]
            for k, rows in enumerate(across(*two)):
                first = pl.multiple_of(layer * 512 + i * 64 + 32 * k, 32)
                weight[pl.ds(first, 32), 128 * m : 128 * m + 128] = rows.astype(bf16)
        return 0

    lax.fori_loop(0, 8, line, 0)


VMEM = pl.BlockSpec(memory_space=pltpu.VMEM)
SMEM = pl.BlockSpec(memory_space=pltpu.SMEM)


class Reduce:
    def __init__(self, place, pack, rows, bufs, sems):
        self.p, self.pack, self.rows, self.half, self.pair = place, pack, rows, rows // 2, rows // 4
        (self.s_out, self.s_in, self.x1_out, self.x1_in, self.y1_out, self.y1_in,
         self.x2_out, self.x2_in, self.y2_out, self.y2_in, self.z_out, self.z_in) = bufs
        self.send_sem, self.s_sems, self.x1_sems, self.y1_sems, self.x2_sems, self.y2_sems, self.z_sems = sems
        self.sent = 0

    def rows_at(self, start, count):
        return pl.ds(pl.multiple_of(start, 16), count)

    def at(self, buf, start, count):
        ref, first = buf
        return ref.at[self.rows_at(first + start, count)]

    def put(self, buf, start, value):
        ref, first = buf
        ref[self.rows_at(first + start, self.pair), :] = value.astype(bf16)

    def read(self, buf, start):
        ref, first = buf
        return ref[self.rows_at(first + start, self.pair), :].astype(f32)

    def move(self, out, into, sems, index, count, peer):
        start = index * count
        return self.copy(self.at(out, start, count), self.at(into, start, count), sems.at[index], peer)

    def copy(self, src, dst, sem, peer):
        return pltpu.make_async_remote_copy(
            src_ref=src, dst_ref=dst, send_sem=self.send_sem.at[0], recv_sem=sem, device_id=peer, device_id_type=MESH
        )

    def sibling_copy(self, z):
        return self.move(self.s_out, self.s_in, self.s_sems, z, 4 * self.rows, self.p.sibling)

    def first_copies(self, z):
        return (
            self.move(self.x1_out, self.x1_in, self.x1_sems, z, 2 * self.half, self.p.x_peer),
            self.move(self.y1_out, self.y1_in, self.y1_sems, z, 2 * self.half, self.p.y_peer),
        )

    def second_copies(self, z):
        return (
            self.move(self.x2_out, self.x2_in, self.x2_sems, z, self.half, self.p.x_peer),
            self.move(self.y2_out, self.y2_in, self.y2_sems, z, self.half, self.p.y_peer),
        )

    def z_copy(self, src, dst, peer_z):
        return self.copy(
            self.at(self.z_out, dst * self.rows, self.rows), self.at(self.z_in, src * self.rows, self.rows),
            self.z_sems.at[src], self.p.z_peer(peer_z),
        )

    def to_sibling(self, z):
        p = self.p
        for rel in range(4):
            owner = p.owner(rel, z, 1 - p.core)

            def put(m, _, rel=rel, owner=owner):
                start = (z * 4 + rel) * self.rows + m * self.pair
                self.put(self.s_out, start, self.pack(owner, m))
                return 0

            lax.fori_loop(0, 4, put, 0)
        self.sibling_copy(z).start()

    def term(self, rel, z, half, m):
        start = (z * 4 + rel) * self.rows + half * self.half + m * self.pair
        return self.pack(self.p.owner(rel, z), half * 2 + m).astype(f32) + self.read(self.s_in, start)

    def first(self, z):
        self.sibling_copy(z).wait_recv()
        for out, half, rels in ((self.x1_out, 0, (1, 3)), (self.y1_out, 1, (2, 3))):
            for n, rel in enumerate(rels):

                def put(m, _, out=out, half=half, rel=rel, n=n):
                    start = (z * 2 + n) * self.half + m * self.pair
                    self.put(out, start, self.term(rel, z, half, m))
                    return 0

                lax.fori_loop(0, 2, put, 0)
        for copy in self.first_copies(z):
            copy.start()

    def second(self, z):
        for copy in self.first_copies(z):
            copy.wait_recv()
        for out, into, half, rel in ((self.y2_out, self.x1_in, 0, 2), (self.x2_out, self.y1_in, 1, 1)):

            def put(m, _, out=out, into=into, half=half, rel=rel):
                there = (z * 2 + 1) * self.half + m * self.pair
                total = self.term(rel, z, half, m) + self.read(into, there)
                self.put(out, z * self.half + m * self.pair, total)
                return 0

            lax.fori_loop(0, 2, put, 0)
        for copy in self.second_copies(z):
            copy.start()

    def column(self, z, half, m):
        first, second = ((self.x1_in, self.y2_in), (self.y1_in, self.x2_in))[half]
        return (
            self.term(0, z, half, m)
            + self.read(first, z * 2 * self.half + m * self.pair)
            + self.read(second, z * self.half + m * self.pair)
        )

    def third(self, z):
        for copy in self.second_copies(z):
            copy.wait_recv()
        for half in range(2):

            def put(m, _, half=half):
                start = z * self.rows + half * self.half + m * self.pair
                self.put(self.z_out, start, self.column(z, half, m))
                return 0

            lax.fori_loop(0, 2, put, 0)
        self.z_copy(self.p.z, z, z).start()

    def last(self, out):
        p = self.p
        for copy in self.second_copies(p.z):
            copy.wait_recv()
        for z in p.others:
            self.z_copy(z, p.z, z).wait_recv()
        for half in range(2):

            def put(m, _, half=half):
                total = self.column(p.z, half, m)
                start = half * self.half + m * self.pair
                for z in p.others:
                    total = total + self.read(self.z_in, z * self.rows + start)
                out[pl.ds(pl.multiple_of(start, 8), self.pair), :] = total
                return 0

            lax.fori_loop(0, 2, put, 0)

    def finish(self):
        whole = self.at((self.s_out[0], 0), 0, 31 * self.rows)
        self.copy(whole, whole, self.z_sems.at[0], self.p.sibling).wait_send()

    def events(self, out, steps):
        order = self.p.others[::-1] + [self.p.z]

        def event(step):
            kind, k = step
            if kind == "last":
                return lambda: self.last(out)
            return lambda: getattr(self, kind)(order[k])

        return [event(step) for step in steps]


def steps_of(*kinds):
    seen = {}
    for kind in kinds:
        seen[kind] = seen.get(kind, -1) + 1
        yield kind, seen[kind]


TO, ONE, TWO, THREE, LAST = "to_sibling", "first", "second", "third", "last"
REDUCE_ORDER = tuple(
    steps_of(TO, TO, ONE, TO, ONE, TO, TWO, ONE, TWO, THREE, TWO, ONE, THREE, THREE, TWO, LAST)
)
REDUCE_ORDER_OUT = tuple(
    steps_of(TO, TO, ONE, TO, ONE, TWO, TO, ONE, TWO, THREE, ONE, TWO, THREE, TWO, THREE, LAST)
)


REDUCE_COUNTS = (16, 4, 4, 2, 2, 4)
REDUCE_SEMS = [pltpu.SemaphoreType.DMA((n,)) for n in (1, 4, 4, 4, 4, 4, 4)]


def reduce_bufs(out, into, rows):
    bufs, first = [], 0
    for count in REDUCE_COUNTS:
        bufs += [(out, first), (into, first)]
        first += count * rows
    return bufs


def pack_in(owner, grad):
    def pack(device, m):
        halves = []
        for h in range(2):
            b = owner[device * 8 + m * 2 + h]
            layer, i, j = lax.div(b, 128), lax.div(lax.rem(b, 128), 8), lax.rem(b, 8)
            halves.append(grad[layer * 8 + j, pl.ds(69 * i, 72), :])
        return jnp.concatenate(halves, axis=0)

    return pack


def pack_out(owner, grad):
    def pack(device, m):
        return jnp.concatenate([grad[owner[device * 8 + m * 2 + h]] for h in range(2)], axis=0)

    return pack


def dot(a, b, ca, cb, precision=None):
    return lax.dot_general(
        a, b, (((ca,), (cb,)), ((), ())), precision=precision, preferred_element_type=f32
    )


def shampoo_block(grad, left, right, root_left, root_right, weight, rate):
    new_left = 0.5 * left + 0.5 * dot(grad, grad, 1, 1, highest)
    new_right = 0.5 * right + 0.5 * dot(grad, grad, 0, 0, highest)
    step = dot(dot(root_left, grad, 1, 0, highest), root_right, 1, 0, highest)
    return new_left, new_right, weight - rate * step


def dot(a, b, ca, cb, precision=None):
    return lax.dot_general(
        a, b, (((ca,), (cb,)), ((), ())), precision=precision, preferred_element_type=f32
    )


def tile(t, size=TILE):
    return pl.ds(pl.multiple_of(t * size, size), size)


def wide(mask):
    return jnp.concatenate([mask, mask], axis=1)


def gate_of(left, right):
    tau = jnp.tanh(left)
    sigma = 0.5 * jnp.tanh(0.5 * right) + 0.5
    hidden = tau * sigma
    return hidden, sigma - hidden * tau, hidden * (1.0 - sigma)


class Planes:
    def __init__(self, ref, samples, count):
        self.ref, self.samples, self.count = ref, samples, count

    def rows(self, plane, start, size):
        return pl.ds(pl.multiple_of(plane * self.samples + start, size), size)

    def get(self, t, planes, size=TILE):
        return jnp.concatenate([self.ref[self.rows(c, t * size, size), :] for c in planes], axis=1)

    def put(self, t, planes, value, size=TILE):
        for n, c in enumerate(planes):
            self.ref[self.rows(c, t * size, size), :] = value[:, 128 * n : 128 * n + 128]


class Layers:
    def __init__(self, refs, place):
        self.__dict__.update(refs)
        self.place = place
        self.samples = self.hidden.shape[0]
        self.tiles = self.samples // TILE
        self.gate = Planes(self.stack_in, self.samples, 8)
        self.early_at = 8 * self.samples


    def make_masks(self):
        def step(t, _):
            pos = self.place.seq * self.samples + t * TILE + lax.broadcasted_iota(i32, (TILE, 128), 0)
            end, start = 0, jnp.zeros((TILE, 128), i32)
            for k in range(self.lengths.shape[1]):
                end = end + self.lengths[0, k]
                start = start + jnp.where(end <= pos, self.lengths[0, k], 0)
            for ref, dilation in ((self.mask_long, FIRST_DILATION), (self.mask_short, 1)):
                ref[tile(t), :] = jnp.where(pos - dilation >= start, 1.0, 0.0).astype(bf16)
            return 0

        lax.fori_loop(0, self.tiles, step, 0)

    def make_inverse(self):
        block = lax.broadcasted_iota(i32, (2, 128), 0) * 128 + lax.broadcasted_iota(i32, (2, 128), 1)

        def step(q, found):
            return jnp.maximum(found, jnp.where(block == self.owner[q], q, 0))

        found = lax.fori_loop(0, 256, step, jnp.zeros((2, 128), i32), unroll=8)
        self.inverse_vmem[pl.ds(0, 2), :] = found
        copy = pltpu.make_async_copy(self.inverse_vmem, self.inverse, self.inverse_sem)
        copy.start()
        copy.wait()

    def make_condition(self):
        def step(t, _):
            lanes = tile(t)
            part = self.cond_t[:, lanes].astype(f32)
            padded = jnp.concatenate([part, jnp.zeros((128 - part.shape[0], TILE), f32)], axis=0)
            turned = padded.T.astype(bf16)
            self.units1[tile(t), 1024:] = turned
            self.units2[tile(t), 1024:] = turned
            return 0

        lax.fori_loop(0, self.tiles, step, 0)

    def make_delayed(self):
        def step(t, _):
            mask = self.mask_long[tile(t), :]
            for c in range(4):
                before = self.units1[tile(t - 1), 512 + 128 * c : 640 + 128 * c]
                self.units1[tile(t), 128 * c : 128 * c + 128] = before * mask
            return 0

        lax.fori_loop(1, self.tiles, step, 0)

    def make_first_delayed(self):
        mask = self.mask_long[pl.ds(0, TILE), :]
        for c in range(4):
            lanes = slice(128 * c, 128 * c + 128)
            self.units1[pl.ds(0, TILE), lanes] = self.halo_signal[:, lanes] * mask


    def forward_one(self, t):
        for c in range(2):
            left, right = self.halves(self.units1[tile(t), :], self.full_in[0], c)
            hidden, by_tanh, by_sigmoid = gate_of(left, right)
            self.hidden[tile(t), 256 * c : 256 * c + 256] = hidden.astype(bf16)
            self.gate.put(t, range(2 * c, 2 * c + 2), by_tanh.astype(bf16))
            self.gate.put(t, range(4 + 2 * c, 6 + 2 * c), by_sigmoid.astype(bf16))

    def halves(self, units, weight, c):
        return [dot(units, weight[:, first : first + 256], 1, 0) for first in (256 * c, 512 + 256 * c)]

    def state_one(self, t):
        mask = self.mask_short[tile(t), :].astype(f32)
        for c in range(2):
            lanes = slice(256 * c, 256 * c + 256)
            out = dot(self.hidden[tile(t), :512], self.full_out[:512, lanes], 1, 0)
            state = self.units1[tile(t), 512 + 256 * c : 768 + 256 * c].astype(f32) + out
            rounded = state.astype(bf16)
            self.units2[tile(t), 512 + 256 * c : 768 + 256 * c] = rounded
            delayed = pltpu.roll(rounded.astype(f32), 1, 0)
            self.last_rows[t, :, lanes] = delayed[:8]
            self.units2[tile(t), lanes] = (delayed * wide(mask)).astype(bf16)

    def mend_delayed(self, t):
        source = self.halo_state if t == 0 else self.last_rows.at[t - 1]
        first = lax.broadcasted_iota(i32, (16, 128), 0) == 0
        mask = self.mask_short[pl.ds(t * TILE, 16), :].astype(f32)
        rows = pl.ds(t * TILE, 16)
        for c in range(4):
            lanes = slice(128 * c, 128 * c + 128)
            row = jnp.broadcast_to(source[0:1, lanes], (16, 128)) * mask
            self.units2[rows, lanes] = jnp.where(first, row, self.units2[rows, lanes].astype(f32)).astype(bf16)

    def layer_two(self, t):
        for c in range(2):
            left, right = self.halves(self.units2[tile(t), :], self.full_in[1], c)
            hidden, by_tanh, by_sigmoid = gate_of(left, right)
            self.hidden[tile(t), 512 + 256 * c : 768 + 256 * c] = hidden.astype(bf16)
            gh = dot(self.go[tile(t), :], self.full_out[512 + 256 * c : 768 + 256 * c, :], 1, 1)
            self.gz[tile(t), 256 * c : 256 * c + 256] = (gh * by_tanh).astype(bf16)
            self.gz[tile(t), 512 + 256 * c : 768 + 256 * c] = (gh * by_sigmoid).astype(bf16)

    def units_two(self, t):
        mask = wide(self.mask_short[tile(t), :].astype(f32))
        last = lax.broadcasted_iota(i32, (TILE, 256), 0) == TILE - 1
        gz = self.gz[tile(t), :]
        for c in range(2):
            lanes = slice(256 * c, 256 * c + 256)
            early = dot(gz, self.full_in[1, lanes, :], 1, 1) * mask
            self.first_rows[t, :, lanes] = early[:8]
            moved = jnp.where(last, 0.0, pltpu.roll(early, TILE - 1, 0))
            here = dot(gz, self.full_in[1, 512 + 256 * c : 768 + 256 * c, :], 1, 1)
            self.gx[tile(t), lanes] = self.go[tile(t), lanes].astype(f32) + here + moved
        self.cond_grad[:, tile(t)] = self.condition_part(gz, 1)

    def condition_part(self, gz, layer):
        part = dot(gz, self.full_in[layer, 1024:, :], 1, 1).T
        return part[: self.cond_grad.shape[0], :]

    def mend_gx(self, t):
        source = self.halo_grad if t == self.tiles - 1 else self.first_rows.at[t + 1]
        last = lax.broadcasted_iota(i32, (8, 512), 0) == 7
        rows = pl.ds((t + 1) * TILE - 8, 8)
        row = jnp.broadcast_to(source[0:1, :], (8, 512))
        self.gx[rows, :] = self.gx[rows, :] + jnp.where(last, row, 0.0)

    def round_gx(self, t):
        self.go[tile(t), :512] = self.gx[tile(t), :].astype(bf16)

    def layer_one_back(self, t):
        for c in range(2):
            gh = dot(self.go[tile(t), :], self.full_out[256 * c : 256 * c + 256, :], 1, 1)
            for part in range(2):
                gate = self.gate.get(t, range(4 * part + 2 * c, 4 * part + 2 * c + 2)).astype(f32)
                first = 512 * part + 256 * c
                self.gz[tile(t), first : first + 256] = (gh * gate).astype(bf16)


    def weight_out(self, layer):
        def step(m, _):
            lanes = pl.ds(pl.multiple_of(layer * 512 + m * 256, 256), 256)
            grad = dot(self.hidden[:, lanes], self.go[...], 0, 0)
            for i in range(4):
                for j in range(8):
                    pair = grad[64 * i : 64 * i + 64, 128 * j : 128 * j + 128]
                    first = layer * 128 + (m * 4 + i) * 16 + 2 * j
                    for k, block in enumerate(across(pair[:32], pair[32:])):
                        self.grad_out[first + k] = block.astype(bf16)
            return 0

        lax.fori_loop(0, 2, step, 0)

    def weight_in(self, layer, units, m):
        rows = pl.ds(pl.multiple_of(384 * m, 384), 384)
        grad = dot(units[:, rows], self.gz[...], 0, 0)
        for j in range(8):
            self.grad_in[layer * 8 + j, rows, :] = grad[:, 128 * j : 128 * j + 128]


    def early_units_one(self):
        mask = wide(self.mask_long[pl.ds(0, TILE), :].astype(f32))
        for c in range(2):
            lanes = slice(256 * c, 256 * c + 256)
            early = dot(self.gz[pl.ds(0, TILE), :], self.full_in[0, lanes, :], 1, 1) * mask
            for k in range(2):
                rows = pl.ds(self.early_at + TILE * (2 * c + k), TILE)
                self.stack_in[rows, :] = early[:, 128 * k : 128 * k + 128].astype(bf16)

    def units_one(self, t):
        gz = self.gz[tile(t), :]
        mask = wide(self.mask_long[tile(t), :].astype(f32))
        for c in range(2):
            lanes = slice(256 * c, 256 * c + 256)
            if t > 0:
                early = dot(gz, self.full_in[0, lanes, :], 1, 1)
                self.gx[tile(t - 1), lanes] = self.gx[tile(t - 1), lanes] + early * mask
            here = dot(gz, self.full_in[0, 512 + 256 * c : 768 + 256 * c, :], 1, 1)
            self.gx[tile(t), lanes] = self.gx[tile(t), lanes] + here
        self.cond_grad[:, tile(t)] = self.cond_grad[:, tile(t)] + self.condition_part(gz, 0)

    def put_out(self, src, dst, sem):
        copy = pltpu.make_async_copy(src, dst, sem)
        copy.start()
        self.pending.append(copy)

    def send_gx(self, t):
        self.units2[tile(t), :512] = self.gx[tile(t), :].astype(bf16)
        self.put_out(self.units2.at[tile(t), pl.ds(0, 512)], self.grad_x.at[tile(t)], self.gx_sems.at[t])

    def outputs(self, n):
        rows = tile(n, 256)
        for c in range(4):
            lanes = slice(256 * c, 256 * c + 256)
            out = dot(self.hidden[rows, :], self.full_out[:, lanes], 1, 0)
            if c < 2:
                out = out + self.units1[rows, 512 + 256 * c : 768 + 256 * c].astype(f32)
            self.go[rows, lanes] = out.astype(bf16)
        self.output_copy(n).start()

    def output_copy(self, n):
        rows = tile(n, 256)
        return pltpu.make_async_copy(self.go.at[rows], self.both.at[rows], self.stage_sems.at[n])

    def drain(self, copies):
        for copy in copies:
            copy.wait()

    def end_gx(self, near, early_halo):
        t = self.tiles - 1
        near.arrived(*early_halo)
        for c in range(4):
            lanes = slice(128 * c, 128 * c + 128)
            late = self.halo_early[pl.ds(TILE * c, TILE), :].astype(f32)
            self.gx[tile(t), lanes] = self.gx[tile(t), lanes] + late
        self.send_gx(t)

    def tail(self, near, early_halo, small, rest_out):
        work = {}
        work[TO, 3] = [lambda: self.units_one(0)]
        work[ONE, 2] = [lambda: self.units_one(1), lambda: self.send_gx(0), lambda: near.sent(*early_halo)]
        work[THREE, 0] = [lambda: self.units_one(2), lambda: self.send_gx(1), lambda: self.outputs(0)]
        work[ONE, 3] = [lambda: self.outputs(1)]
        work[THREE, 1] = [lambda: self.outputs(2), *rest_out, lambda: small[1].start()]
        work[THREE, 2] = [
            lambda: self.units_one(3),
            lambda: self.send_gx(2),
            lambda: self.end_gx(near, early_halo),
            lambda: small[0].start(),
            lambda: self.outputs(3),
        ]
        work[TWO, 3] = [lambda: loop(4, self.samples // 256, self.outputs)]
        return [work.get(step, []) for step in REDUCE_ORDER]


def loop(first, last, body):
    lax.fori_loop(first, last, lambda t, _: (body(t), 0)[1], 0)


class Neighbours:
    def __init__(self, place):
        self.p = place
        self.has = {1: place.seq < 7, -1: place.seq > 0}

    def copy(self, src, dst, sems, way):
        return pltpu.make_async_remote_copy(
            src_ref=src, dst_ref=dst, send_sem=sems[0], recv_sem=sems[1],
            device_id=(self.p.row, self.p.seq + way), device_id_type=MESH)

    def start(self, src, dst, sems, way):
        pl.when(self.has[way])(lambda: self.copy(src, dst, sems, way).start())

    def sent(self, src, dst, sems, way):
        pl.when(self.has[way])(lambda: self.copy(src, dst, sems, way).wait_send())

    def arrived(self, src, dst, sems, way):
        pl.when(self.has[-way])(lambda: self.copy(src, dst, sems, way).wait_recv())


INPUTS = ("owner", "lengths", "signal", "cot_x", "cot_skip", "cond_t", "w_in", "w_out")
OUTPUTS = ("both", "grad_x", "grad_cond_t", "sum_in", "sum_out")
SCRATCH = dict(
    stack_in=pltpu.VMEM((32 * ROWS_IN, 128), bf16),
    stack_out=pltpu.VMEM((32 * ROWS_OUT, 128), bf16),
    full_in=pltpu.VMEM((2, 1152, 1024), bf16),
    full_out=pltpu.VMEM((1024, 1024), bf16),
    units1=pltpu.VMEM((2048, 1152), bf16),
    units2=pltpu.VMEM((2048, 1152), bf16),
    hidden=pltpu.VMEM((2048, 1024), bf16),
    gz=pltpu.VMEM((2048, 1024), bf16),
    go=pltpu.VMEM((2048, 1024), bf16),
    gx=pltpu.VMEM((2048, 512), f32),
    grad_in=pltpu.VMEM((16, 1152, 128), f32),
    grad_out=pltpu.VMEM((256, 32, 128), bf16),
    mask_long=pltpu.VMEM((2048, 128), bf16),
    mask_short=pltpu.VMEM((2048, 128), bf16),
    halo_signal=pltpu.VMEM((TILE, 512), bf16),
    halo_early=pltpu.VMEM((4 * TILE, 128), bf16),
    last_rows=pltpu.VMEM((4, 8, 512), f32),
    first_rows=pltpu.VMEM((4, 8, 512), f32),
    halo_state=pltpu.VMEM((8, 512), f32),
    halo_grad=pltpu.VMEM((8, 512), f32),
    reduce_in=pltpu.VMEM((32 * ROWS_IN, 128), bf16),
    reduce_out=pltpu.VMEM((32 * ROWS_OUT, 128), bf16),
    cond_grad=pltpu.VMEM((80, 2048), f32),
    share_in=pltpu.VMEM((ROWS_IN, 128), f32),
    share_out=pltpu.VMEM((ROWS_OUT, 128), f32),
    small_sems=pltpu.SemaphoreType.DMA((3,)),
    inverse_vmem=pltpu.VMEM((8, 128), i32),
    inverse=pltpu.SMEM((8, 128), i32),
    inverse_sem=pltpu.SemaphoreType.DMA,
    load_sems=pltpu.SemaphoreType.DMA((3,)),
    gx_sems=pltpu.SemaphoreType.DMA((4,)),
    stage_sems=pltpu.SemaphoreType.DMA((8,)),
    halo_sems=pltpu.SemaphoreType.DMA((8,)),
)


def network_kernel(*refs):
    names = INPUTS + OUTPUTS + tuple(SCRATCH)
    sems = refs[len(names) :]
    gather_sems, reduce_sems = len(GATHER_SEMS), len(REDUCE_SEMS)
    sems_in, sems = sems[:gather_sems], sems[gather_sems:]
    sems_out, sems = sems[:gather_sems], sems[gather_sems:]
    sum_sems_out, sum_sems_in = sems[:reduce_sems], sems[reduce_sems:]
    place = Place()
    n = Layers(dict(zip(names, refs)), place)
    n.pending = []
    near = Neighbours(place)
    samples, tiles = n.samples, n.tiles

    targets = ((n.signal, n.units1, 512), (n.cot_x, n.go, 0), (n.cot_skip, n.go, 512))
    loads = [
        pltpu.make_async_copy(src, dst.at[:, pl.ds(lane, 512)], n.load_sems.at[k])
        for k, (src, dst, lane) in enumerate(targets)
    ]
    for copy in loads:
        copy.start()
    place.announce()
    me = place.row * 8 + place.seq
    pairs_in, blocks_out = n.stack_in.reshape(128, 144, 128), n.stack_out.reshape(256, 32, 128)
    spread = n.grad_in
    spread[0, :ROWS_IN, :] = jnp.zeros((ROWS_IN, 128), f32)
    spread[1, : 8 * 69, :] = n.w_in[...]
    for k in range(8):
        spread[0, pl.ds(72 * k, 69), :] = spread[1, pl.ds(k, 72, 8), :][:69]
    for m in range(4):
        pairs_in[me * 4 + m] = spread[0, 144 * m : 144 * m + 144, :].astype(bf16)

    for k in range(8):
        block = n.w_out[k]
        blocks_out[me * 8 + k] = jnp.concatenate([block[:32], block[32:]], axis=1).astype(bf16)

    def cleared(refs, when):
        @pl.when(when)
        def _():
            for ref in refs:
                ref[...] = jnp.zeros_like(ref)

    cleared([n.halo_signal, n.halo_state], place.seq == 0)
    cleared([n.halo_early, n.halo_grad], place.seq == 7)
    n.make_masks()
    n.make_inverse()
    n.make_condition()
    n.full_in[0, 1104:, :] = jnp.zeros((48, 1024), bf16)
    n.full_in[1, 1104:, :] = jnp.zeros((48, 1024), bf16)
    place.all_here()

    halo = [(n.halo_sems.at[2 * k], n.halo_sems.at[2 * k + 1]) for k in range(4)]
    signal_halo = (n.signal.at[pl.ds(samples - TILE, TILE)], n.halo_signal, halo[0], 1)
    state_halo = (n.last_rows.at[tiles - 1], n.halo_state, halo[1], 1)
    grad_halo = (n.first_rows.at[0], n.halo_grad, halo[2], -1)
    early_halo = (n.stack_in.at[pl.ds(n.early_at, 4 * TILE)], n.halo_early, halo[3], -1)
    into = Gather(place, pairs_in, 4, sems_in)
    out = Gather(place, blocks_out, 8, sems_out)
    order = [place.z] + place.others
    into.start()
    into.start_sides()
    out.start()
    for k in range(3):
        into.along_z(k)
        out.relay(k, 0)
        out.relay(k, 1)
        into.first(order[k])
    into.rest(order[0])
    into.first(order[3])
    near.start(*signal_halo)
    out.start_sides()
    for k in range(3):
        out.spread(k, 0)
        out.spread(k, 1)
    for copy in loads:
        copy.wait()
    n.make_delayed()
    for k in range(1, tiles):
        into.rest(order[k])
    into.finish()
    assemble_in(n.inverse, pairs_in, spread, n.full_in, 0)
    assemble_in(n.inverse, pairs_in, spread, n.full_in, 1)

    near.arrived(*signal_halo)
    n.make_first_delayed()
    out.first(order[0])
    out.first(order[1])
    loop(0, 2, n.forward_one)
    out.first(order[2])
    out.first(order[3])
    out.rest(order[0])
    out.rest(order[1])
    loop(2, tiles, n.forward_one)
    out.rest(order[2])
    out.rest(order[3])
    out.finish()
    assemble_out(n.inverse, blocks_out, n.full_out, 0)
    assemble_out(n.inverse, blocks_out, n.full_out, 1)
    n.state_one(tiles - 1)
    near.start(*state_halo)
    loop(0, tiles - 1, n.state_one)
    for t in range(1, tiles):
        n.mend_delayed(t)
    near.arrived(*state_halo)
    n.mend_delayed(0)

    loop(0, tiles, n.layer_two)
    n.units_two(0)
    near.start(*grad_halo)
    loop(1, tiles, n.units_two)
    n.weight_out(1)
    for t in range(tiles - 1):
        n.mend_gx(t)
    near.arrived(*grad_halo)
    n.mend_gx(tiles - 1)
    loop(0, tiles, n.round_gx)
    n.weight_out(0)

    reduce_out = Reduce(
        place, pack_out(n.owner, n.grad_out), ROWS_OUT,
        reduce_bufs(n.stack_out, n.reduce_out, ROWS_OUT), sum_sems_out,
    )
    reduce_in = Reduce(
        place, pack_in(n.owner, n.grad_in), ROWS_IN,
        reduce_bufs(n.stack_in, n.reduce_in, ROWS_IN), sum_sems_in,
    )
    sum_out = reduce_out.events(n.share_out, REDUCE_ORDER_OUT)
    sum_in = reduce_in.events(n.share_in, REDUCE_ORDER)

    def run(*events):
        for event in events:
            event()

    small = [
        pltpu.make_async_copy(a, b, n.small_sems.at[k])
        for k, (a, b) in enumerate(
            ((n.cond_grad, n.grad_cond_t), (n.share_out, n.sum_out), (n.share_in, n.sum_in))
        )
    ]
    run(*sum_out[:2])
    n.weight_in(1, n.units2, 0)
    run(*sum_out[2:5], sum_out[6])
    n.weight_in(1, n.units2, 1)
    run(sum_out[5], sum_out[7])
    n.weight_in(1, n.units2, 2)
    run(*sum_out[8:10])
    loop(0, 2, n.layer_one_back)
    run(*sum_out[10:12])
    loop(2, tiles, n.layer_one_back)
    run(*sum_out[12:14])
    n.early_units_one()
    near.start(*early_halo)
    n.weight_in(0, n.units1, 0)
    run(sum_out[14])
    n.weight_in(0, n.units1, 1)
    n.weight_in(0, n.units1, 2)
    for event, work in zip(sum_in, n.tail(near, early_halo, small, [sum_out[15], reduce_out.finish])):
        event()
        for part in work:
            part()
    reduce_in.finish()
    small[2].start()
    for halo in (signal_halo, state_halo, grad_halo):
        near.sent(*halo)
    n.drain(n.pending)
    loop(0, samples // 256, lambda k: n.output_copy(k).wait())
    n.drain(small)


ANY = pl.BlockSpec(memory_space=pl.ANY)


def shampoo_block(grad, left, right, root_left, root_right, weight, rate):
    low = grad.astype(bf16)
    new_left = 0.5 * left + 0.5 * dot(low, low, 1, 1)
    new_right = 0.5 * right + 0.5 * dot(low, low, 0, 0)
    step = dot(dot(root_left.astype(bf16), low, 1, 0).astype(bf16), root_right.astype(bf16), 1, 0)
    return new_left, new_right, weight - rate * step


BLOCKS_IN = ("w_in", "left_in", "root_left_in", "right_in", "root_right_in")
BLOCKS_OUT = ("w_out", "left_out", "root_left_out", "right_out", "root_right_out")
SUMS = ("sum_in", "sum_out")
LARGE = ("out_x", "skip_sum", "grad_x")
LOW = ("both", "grad_x")


def finish_kernel(*refs):
    taken = SUMS + BLOCKS_IN + BLOCKS_OUT
    names = ["from_" + a for a in taken + LOW + ("cond",)]
    names += ["to_" + a for a in LARGE + ("cond", "grad_in", "grad_out")]
    names += ["to_" + a for kind in ("in", "out") for a in ("w_" + kind, "left_" + kind, "right_" + kind)]
    names += list(taken) + ["grad_in", "grad_out", "large", "both", "low", "cond", "load_sems", "store_sems"]
    r = dict(zip(names, refs))
    loads, stores, sems = {}, {}, iter(range(64))

    def move(table, key, src, dst, sem):
        table[key] = pltpu.make_async_copy(src, dst, r[sem].at[next(sems)])

    for a in taken:
        there = r[a].at[pl.ds(0, 552)] if a in BLOCKS_IN[:3] else r[a]
        move(loads, a, r["from_" + a], there, "load_sems")
    for m in range(4):
        move(loads, ("both", m), r["from_both"].at[tile(m)], r["both"].at[tile(m)], "load_sems")
        move(loads, ("low", m), r["from_grad_x"].at[tile(m)], r["low"].at[tile(m)], "load_sems")
    move(loads, "cond", r["from_cond"], r["cond"], "load_sems")
    sems = iter(range(64))
    for m in range(4):
        for k in range(3):
            move(stores, (k, m), r["large"].at[k, tile(m)], r["to_" + LARGE[k]].at[tile(m)], "store_sems")
    for a in ("cond", "grad_in", "w_in", "left_in", "right_in", "grad_out", "w_out", "left_out", "right_out"):
        here = r[a].at[pl.ds(0, 552)] if a in ("grad_in", "w_in", "left_in") else r[a]
        move(stores, a, here, r["to_" + a], "store_sems")
    for copy in loads.values():
        copy.start()

    def widen(m, name):
        loads[name, m].wait()
        for k in (0, 1) if name == "both" else (2,):
            lanes = slice(512 * (k % 2), 512 * (k % 2) + 512)
            r["large"][k, tile(m), :] = r[name][tile(m), lanes].astype(f32)
            stores[k, m].start()

    for a in ("sum_in",) + BLOCKS_IN:
        loads[a].wait()
    for k in range(8):
        at, put = pl.ds(k, 72, 8), pl.ds(k, 69, 8)
        grad = r["sum_in"][72 * k : 72 * k + 72, :]
        r["grad_in"][at, :] = grad
        r["left_in"][put, :], r["right_in"][k], r["w_in"][put, :] = shampoo_block(
            grad[:69], r["left_in"][at, :][:69], r["right_in"][k], r["root_left_in"][at, :][:69],
            r["root_right_in"][k], r["w_in"][at, :][:69], rate_in,
        )
        if k % 2 == 0:
            widen(k // 2, "both")
    for a in ("grad_in", "w_in", "left_in", "right_in"):
        stores[a].start()
    for a in ("sum_out", "cond") + BLOCKS_OUT:
        loads[a].wait()
    stores["cond"].start()
    for k in range(8):
        folded = r["sum_out"][32 * k : 32 * k + 32, :]
        grad = jnp.concatenate([folded[:, :64], folded[:, 64:]], axis=0)
        r["grad_out"][k] = grad
        r["left_out"][k], r["right_out"][k], r["w_out"][k] = shampoo_block(
            grad, r["left_out"][k], r["right_out"][k], r["root_left_out"][k], r["root_right_out"][k],
            r["w_out"][k], rate_out,
        )
        if k % 2 == 0:
            widen(k // 2, "low")
    for a in ("grad_out", "w_out", "left_out", "right_out"):
        stores[a].start()
    for copy in stores.values():
        copy.wait()


def rows_first(blocks):
    return blocks.transpose(1, 0, 2)


def fused_local(
    signal, condition, lengths, owner, grad_out, grad_skip, w_in, w_out,
    left_in, right_in, root_left_in, root_right_in,
    left_out, right_out, root_left_out, root_right_out,
):
    samples, width, mels = signal.shape[1], signal.shape[2], condition.shape[2]
    block = lambda *shape: jax.ShapeDtypeStruct(shape, f32)
    low = [jax.ShapeDtypeStruct((samples, lanes), bf16) for lanes in (2 * width, width)]
    large = [block(samples, width)] * 3 + [block(mels, samples)]
    rows_in = rows_first(w_in).reshape(552, 128)
    both, grad_x, grad_cond_t, sum_in, sum_out = pl.pallas_call(
        network_kernel,
        out_shape=low + [block(mels, samples), block(ROWS_IN, 128), block(ROWS_OUT, 128)],
        in_specs=[SMEM, SMEM, ANY, ANY, ANY, VMEM, VMEM, VMEM],
        out_specs=[ANY] * 5,
        scratch_shapes=list(SCRATCH.values()) + GATHER_SEMS * 2 + REDUCE_SEMS * 2,
        name="network",
        compiler_params=pltpu.CompilerParams(
            collective_id=0, has_side_effects=True, vmem_limit_bytes=64 << 20
        ),
    )(
        owner, lengths, signal[0], grad_out[0], grad_skip[0], condition[0].T, rows_in, w_out,
    )
    taken = (
        sum_in, sum_out,
        rows_in, rows_first(left_in).reshape(552, 69), rows_first(root_left_in).reshape(552, 69),
        right_in, root_right_in,
        w_out, left_out, root_left_out, right_out, root_right_out,
    )
    new_in = [block(552, 128), block(552, 69), block(8, 128, 128)]
    new_out = [block(8, 64, 64)] * 3
    held = [pltpu.VMEM((584 if a.shape[0] == 552 else a.shape[0], *a.shape[1:]), f32) for a in taken]
    outs = pl.pallas_call(
        finish_kernel,
        out_shape=large + [new_in[0], new_out[0]] + new_in + new_out,
        in_specs=[ANY] * (len(taken) + 3),
        out_specs=[ANY] * 12,
        scratch_shapes=held
        + [pltpu.VMEM((584, 128), f32), pltpu.VMEM((8, 64, 64), f32)]
        + [pltpu.VMEM((3, samples, width), f32)]
        + [pltpu.VMEM(a.shape, a.dtype) for a in low + [block(mels, samples)]]
        + [pltpu.SemaphoreType.DMA((32,))] * 2,
        name="finish",
        compiler_params=pltpu.CompilerParams(vmem_limit_bytes=63 << 20),
    )(*taken, both, grad_x, grad_cond_t)
    out_x, skip_sum, grad_x, grad_cond_t, g_in, g_out, nw_in, nl_in, nr_in, nw_out, nl_out, nr_out = outs

    def blocks_first(rows):
        return rows.reshape(69, 8, rows.shape[1]).transpose(1, 0, 2)

    return (
        out_x[None], skip_sum[None], grad_x[None], grad_cond_t.T[None],
        blocks_first(g_in), g_out, blocks_first(nl_in), nr_in, nl_out, nr_out, blocks_first(nw_in), nw_out,
    )


def local(
    signal,
    condition,
    lengths,
    owner,
    grad_out,
    grad_skip,
    w_in,
    w_out,
    left_in,
    right_in,
    root_left_in,
    root_right_in,
    left_out,
    right_out,
    root_left_out,
    root_right_out,
):
    fused = (lax.axis_size("row"), lax.axis_size("seq"), signal.shape[1]) == (4, 8, 4 * TILE)
    audio_samples = signal.shape[1]
    width = signal.shape[2]
    if fused:
        return fused_local(
            signal, condition, lengths, owner, grad_out, grad_skip, w_in, w_out,
            left_in, right_in, root_left_in, root_right_in,
            left_out, right_out, root_left_out, root_right_out,
        )
    stack_in = lax.all_gather(w_in.astype(bf16), ("row", "seq"), axis=0, tiled=True)
    stack_out = lax.all_gather(w_out.astype(bf16), ("row", "seq"), axis=0, tiled=True)
    inverse = jnp.argsort(owner)
    input_weight = from_blocks(jnp.take(stack_in, inverse, axis=0), 16, 8)
    output_weight = from_blocks(jnp.take(stack_out, inverse, axis=0), 8, 16)
    sample_positions = lax.axis_index("seq") * audio_samples + jnp.arange(
        audio_samples, dtype=jnp.int32
    )
    longer_mask = receptive_mask(lengths, sample_positions, FIRST_DILATION)[:, :, None]
    mask_short = receptive_mask(lengths, sample_positions, 1)[:, :, None]
    preceding_longer = shifted(signal[:, audio_samples - FIRST_DILATION :, :], "seq", 1)
    delayed_one = jnp.concatenate([preceding_longer, signal], axis=1)[:, :audio_samples, :]
    delayed_one = jnp.where(longer_mask, delayed_one, jnp.zeros_like(delayed_one))
    units_one = jnp.concatenate([delayed_one, signal, condition], axis=2)
    tanh_one, sigm_one, hidden_one, proj_one = gate_forward(
        units_one, input_weight[0], output_weight[0]
    )
    first_layer_state = signal.astype(jnp.float32) + proj_one[..., :width]
    rounded_one = first_layer_state.astype(jnp.bfloat16)
    before_short = shifted(rounded_one[:, audio_samples - 1 :, :], "seq", 1)
    delayed_two = jnp.concatenate([before_short, rounded_one[:, : audio_samples - 1, :]], axis=1)
    delayed_two = jnp.where(mask_short, delayed_two, jnp.zeros_like(delayed_two))
    units_two = jnp.concatenate([delayed_two, rounded_one, condition], axis=2)
    tanh_two, sigm_two, hidden_two, proj_two = gate_forward(
        units_two, input_weight[1], output_weight[1]
    )
    out_x = first_layer_state + proj_two[..., :width]
    skip_sum = proj_one[..., width:] + proj_two[..., width:]
    grad_next = grad_out.astype(jnp.float32)
    gin_two, gout_two, units_grad_two = gate_backward(
        units_two,
        tanh_two,
        sigm_two,
        hidden_two,
        input_weight[1],
        output_weight[1],
        grad_next,
        grad_skip,
    )
    early_two = jnp.where(mask_short, units_grad_two[..., :width], 0.0)
    from_short = shifted(early_two[:, :1, :], "seq", -1)
    grad_state = (
        grad_next
        + units_grad_two[..., width : 2 * width]
        + jnp.concatenate([early_two[:, 1:, :], from_short], axis=1)
    )
    gin_one, gout_one, units_grad_one = gate_backward(
        units_one,
        tanh_one,
        sigm_one,
        hidden_one,
        input_weight[0],
        output_weight[0],
        grad_state,
        grad_skip,
    )
    earlier_first = jnp.where(longer_mask, units_grad_one[..., :width], 0.0)
    taken_longer = shifted(earlier_first[:, :FIRST_DILATION, :], "seq", -1)
    grad_x = (
        grad_state
        + units_grad_one[..., width : 2 * width]
        + jnp.concatenate([earlier_first[:, FIRST_DILATION:, :], taken_longer], axis=1)
    )
    grad_cond = units_grad_one[..., 2 * width :] + units_grad_two[..., 2 * width :]
    local_in = jnp.take(to_blocks(jnp.stack([gin_one, gin_two]), 16, 8), owner, axis=0)
    local_out = jnp.take(to_blocks(jnp.stack([gout_one, gout_two]), 8, 16), owner, axis=0)
    grad_in_blocks, grad_out_blocks = (
        lax.psum_scatter(local_in, ("row", "seq"), scatter_dimension=0, tiled=True),
        lax.psum_scatter(local_out, ("row", "seq"), scatter_dimension=0, tiled=True),
    )
    new_left_in, new_right_in, new_w_in = shampoo(
        grad_in_blocks, left_in, right_in, root_left_in, root_right_in, w_in, rate_in
    )
    new_left_out, new_right_out, new_w_out = shampoo(
        grad_out_blocks, left_out, right_out, root_left_out, root_right_out, w_out, rate_out
    )
    return (
        out_x,
        skip_sum,
        grad_x,
        grad_cond,
        grad_in_blocks,
        grad_out_blocks,
        new_left_in,
        new_right_in,
        new_left_out,
        new_right_out,
        new_w_in,
        new_w_out,
    )


def solution(mesh):
    tokens, blocks = P("row", "seq", None), P(("row", "seq"), None, None)
    in_specs = (tokens, tokens, P("row", None), P(), tokens, tokens) + (blocks,) * 10
    out_specs = (tokens,) * 4 + (blocks,) * 8
    return jax.shard_map(local, mesh=mesh, in_specs=in_specs, out_specs=out_specs, check_vma=False)
```

profile of v0, /device:TPU:0, one launch (start us, length us, event | category | flops | bytes accessed | tf_op | source)
XLA Modules:
  0.0 125.0 jit_solution(3195227928048914819)
XLA Ops:
  0.6 115.0 %network.1 = (bf16[2048,1024]{1,0:T(8,128)(2,1)}, bf16[2048,512]{1,0:T(8,128)(2,1)}, f32[80,2048]{1,0:T(8,128)}, f32[576,128]{1,0:T(8,128)}, f32[256,128]{1,0:T(8,128)}) custom-call(s32[256]{0:T(256)} %refs_0_.1, s32[1,4]{1,0:T(1,128)} %refs_1_.1, bf16[2048,512]{1,0:T(8,128)(2,1)} %bitcast.30, bf16[2048,512]{1,0:T(8,128)(2,1)} %bitcast.31, ...), custom_call_target="tpu_custom_call" | custom-call | tf_op jit(solution)/shard_map/network/pallas_call | solution.py:1111
  115.7 9.1 %finish.1 = (f32[2048,512]{1,0:T(8,128)}, f32[2048,512]{1,0:T(8,128)}, f32[2048,512]{1,0:T(8,128)}, f32[80,2048]{1,0:T(8,128)}, f32[552,128]{1,0:T(8,128)}, /*in...) custom-call(f32[576,128]{1,0:T(8,128)} %get-tuple-element.29.refs_0_, ...), custom_call_target="tpu_custom_call" | custom-call | tf_op jit(solution)/shard_map/finish/pallas_call | solution.py:1133
where the time goes:
time: 126 us; the launch traced here: 125 us
  Pallas kernels  124 us (98%)
    pallas_call x1, Pallas kernels, fused_local(): pl.pallas_call(network_kernel, out_shape=low + [block(mels, samples), blo...  115 us
    pallas_call x1, Pallas kernels, fused_local(): pl.pallas_call(finish_kernel, out_shape=large + [new_in[0], new_out[0]] +...  9.07 us

commit v1 on v0

--- a/solution.py
+++ b/solution.py
@@ -454,7 +454,7 @@
     steps_of(TO, TO, ONE, TO, ONE, TO, TWO, ONE, TWO, THREE, TWO, ONE, THREE, THREE, TWO, LAST)
 )
 REDUCE_ORDER_OUT = tuple(
-    steps_of(TO, TO, ONE, TO, ONE, TWO, TO, ONE, TWO, THREE, ONE, TWO, THREE, TWO, THREE, LAST)
+    steps_of(TO, TO, ONE, TO, ONE, TO, ONE, ONE, TWO, TWO, TWO, THREE, TWO, THREE, THREE, LAST)
 )
 
 
@@ -760,8 +760,9 @@
 
     def tail(self, near, early_halo, small, rest_out):
         work = {}
-        work[TO, 3] = [lambda: self.units_one(0)]
-        work[ONE, 2] = [lambda: self.units_one(1), lambda: self.send_gx(0), lambda: near.sent(*early_halo)]
+        work[TO, 3] = [self.early_units_one, lambda: near.start(*early_halo), lambda: self.units_one(0)]
+        work[ONE, 2] = [lambda: self.units_one(1), lambda: self.send_gx(0)]
+        work[TWO, 1] = [lambda: near.sent(*early_halo)]
         work[THREE, 0] = [lambda: self.units_one(2), lambda: self.send_gx(1), lambda: self.outputs(0)]
         work[ONE, 3] = [lambda: self.outputs(1)]
         work[THREE, 1] = [lambda: self.outputs(2), *rest_out, lambda: small[1].start()]
@@ -770,9 +771,8 @@
             lambda: self.send_gx(2),
             lambda: self.end_gx(near, early_halo),
             lambda: small[0].start(),
-            lambda: self.outputs(3),
         ]
-        work[TWO, 3] = [lambda: loop(4, self.samples // 256, self.outputs)]
+        work[TWO, 3] = [lambda: loop(3, self.samples // 256, self.outputs)]
         return [work.get(step, []) for step in REDUCE_ORDER]
 
 
@@ -800,7 +800,7 @@
         pl.when(self.has[-way])(lambda: self.copy(src, dst, sems, way).wait_recv())
 
 
-INPUTS = ("owner", "lengths", "signal", "cot_x", "cot_skip", "cond_t", "w_in", "w_out")
+INPUTS = ("owner", "lengths", "signal", "cot_x", "cot_skip", "from_cond", "from_w_in", "from_w_out")
 OUTPUTS = ("both", "grad_x", "grad_cond_t", "sum_in", "sum_out")
 SCRATCH = dict(
     stack_in=pltpu.VMEM((32 * ROWS_IN, 128), bf16),
@@ -825,6 +825,9 @@
     halo_grad=pltpu.VMEM((8, 512), f32),
     reduce_in=pltpu.VMEM((32 * ROWS_IN, 128), bf16),
     reduce_out=pltpu.VMEM((32 * ROWS_OUT, 128), bf16),
+    cond_t=pltpu.VMEM((80, 2048), bf16),
+    w_in=pltpu.VMEM((552, 128), f32),
+    w_out=pltpu.VMEM((8, 64, 64), f32),
     cond_grad=pltpu.VMEM((80, 2048), f32),
     share_in=pltpu.VMEM((ROWS_IN, 128), f32),
     share_out=pltpu.VMEM((ROWS_OUT, 128), f32),
@@ -832,7 +835,7 @@
     inverse_vmem=pltpu.VMEM((8, 128), i32),
     inverse=pltpu.SMEM((8, 128), i32),
     inverse_sem=pltpu.SemaphoreType.DMA,
-    load_sems=pltpu.SemaphoreType.DMA((3,)),
+    load_sems=pltpu.SemaphoreType.DMA((6,)),
     gx_sems=pltpu.SemaphoreType.DMA((4,)),
     stage_sems=pltpu.SemaphoreType.DMA((8,)),
     halo_sems=pltpu.SemaphoreType.DMA((8,)),
@@ -852,17 +855,24 @@
     near = Neighbours(place)
     samples, tiles = n.samples, n.tiles
 
+    place.announce()
     targets = ((n.signal, n.units1, 512), (n.cot_x, n.go, 0), (n.cot_skip, n.go, 512))
+    early = [
+        pltpu.make_async_copy(src, dst, n.load_sems.at[k])
+        for k, (src, dst) in enumerate(
+            ((n.from_w_in, n.w_in), (n.from_w_out, n.w_out), (n.from_cond, n.cond_t))
+        )
+    ]
     loads = [
-        pltpu.make_async_copy(src, dst.at[:, pl.ds(lane, 512)], n.load_sems.at[k])
+        pltpu.make_async_copy(src, dst.at[:, pl.ds(lane, 512)], n.load_sems.at[3 + k])
         for k, (src, dst, lane) in enumerate(targets)
     ]
-    for copy in loads:
+    for copy in early + loads:
         copy.start()
-    place.announce()
     me = place.row * 8 + place.seq
     pairs_in, blocks_out = n.stack_in.reshape(128, 144, 128), n.stack_out.reshape(256, 32, 128)
     spread = n.grad_in
+    early[0].wait()
     spread[0, :ROWS_IN, :] = jnp.zeros((ROWS_IN, 128), f32)
     spread[1, : 8 * 69, :] = n.w_in[...]
     for k in range(8):
@@ -870,6 +880,7 @@
     for m in range(4):
         pairs_in[me * 4 + m] = spread[0, 144 * m : 144 * m + 144, :].astype(bf16)
 
+    early[1].wait()
     for k in range(8):
         block = n.w_out[k]
         blocks_out[me * 8 + k] = jnp.concatenate([block[:32], block[32:]], axis=1).astype(bf16)
@@ -882,11 +893,6 @@
 
     cleared([n.halo_signal, n.halo_state], place.seq == 0)
     cleared([n.halo_early, n.halo_grad], place.seq == 7)
-    n.make_masks()
-    n.make_inverse()
-    n.make_condition()
-    n.full_in[0, 1104:, :] = jnp.zeros((48, 1024), bf16)
-    n.full_in[1, 1104:, :] = jnp.zeros((48, 1024), bf16)
     place.all_here()
 
     halo = [(n.halo_sems.at[2 * k], n.halo_sems.at[2 * k + 1]) for k in range(4)]
@@ -900,8 +906,18 @@
     into.start()
     into.start_sides()
     out.start()
-    for k in range(3):
+
+    def make_rest():
+        early[2].wait()
+        n.make_condition()
+        n.full_in[0, 1104:, :] = jnp.zeros((48, 1024), bf16)
+        n.full_in[1, 1104:, :] = jnp.zeros((48, 1024), bf16)
+
+    n.make_masks()
+    n.make_inverse()
+    for k, work in enumerate((make_rest, lambda: None, lambda: None)):
         into.along_z(k)
+        work()
         out.relay(k, 0)
         out.relay(k, 1)
         into.first(order[k])
@@ -979,19 +995,17 @@
     ]
     run(*sum_out[:2])
     n.weight_in(1, n.units2, 0)
-    run(*sum_out[2:5], sum_out[6])
+    run(*sum_out[2:6])
     n.weight_in(1, n.units2, 1)
-    run(sum_out[5], sum_out[7])
+    run(*sum_out[6:8])
     n.weight_in(1, n.units2, 2)
     run(*sum_out[8:10])
     loop(0, 2, n.layer_one_back)
-    run(*sum_out[10:12])
+    run(sum_out[10])
     loop(2, tiles, n.layer_one_back)
-    run(*sum_out[12:14])
-    n.early_units_one()
-    near.start(*early_halo)
+    run(*sum_out[11:13])
     n.weight_in(0, n.units1, 0)
-    run(sum_out[14])
+    run(*sum_out[13:15])
     n.weight_in(0, n.units1, 1)
     n.weight_in(0, n.units1, 2)
     for event, work in zip(sum_in, n.tail(near, early_halo, small, [sum_out[15], reduce_out.finish])):
@@ -1061,7 +1075,7 @@
             r["large"][k, tile(m), :] = r[name][tile(m), lanes].astype(f32)
             stores[k, m].start()
 
-    for a in ("sum_in",) + BLOCKS_IN:
+    for a in taken:
         loads[a].wait()
     for k in range(8):
         at, put = pl.ds(k, 72, 8), pl.ds(k, 69, 8)
@@ -1071,14 +1085,6 @@
             grad[:69], r["left_in"][at, :][:69], r["right_in"][k], r["root_left_in"][at, :][:69],
             r["root_right_in"][k], r["w_in"][at, :][:69], rate_in,
         )
-        if k % 2 == 0:
-            widen(k // 2, "both")
-    for a in ("grad_in", "w_in", "left_in", "right_in"):
-        stores[a].start()
-    for a in ("sum_out", "cond") + BLOCKS_OUT:
-        loads[a].wait()
-    stores["cond"].start()
-    for k in range(8):
         folded = r["sum_out"][32 * k : 32 * k + 32, :]
         grad = jnp.concatenate([folded[:, :64], folded[:, 64:]], axis=0)
         r["grad_out"][k] = grad
@@ -1086,8 +1092,12 @@
             grad, r["left_out"][k], r["right_out"][k], r["root_left_out"][k], r["root_right_out"][k],
             r["w_out"][k], rate_out,
         )
-        if k % 2 == 0:
+        if k % 2:
+            widen(k // 2, "both")
             widen(k // 2, "low")
+    loads["cond"].wait()
+    for a in ("cond", "grad_in", "w_in", "left_in", "right_in"):
+        stores[a].start()
     for a in ("grad_out", "w_out", "left_out", "right_out"):
         stores[a].start()
     for copy in stores.values():
@@ -1111,7 +1121,7 @@
     both, grad_x, grad_cond_t, sum_in, sum_out = pl.pallas_call(
         network_kernel,
         out_shape=low + [block(mels, samples), block(ROWS_IN, 128), block(ROWS_OUT, 128)],
-        in_specs=[SMEM, SMEM, ANY, ANY, ANY, VMEM, VMEM, VMEM],
+        in_specs=[SMEM, SMEM] + [ANY] * 6,
         out_specs=[ANY] * 5,
         scratch_shapes=list(SCRATCH.values()) + GATHER_SEMS * 2 + REDUCE_SEMS * 2,
         name="network",

time: 126 us -> 123 us (0.976)
  Pallas kernels: 124 us -> 122 us
    pallas_call x1, Pallas kernels: 115 us -> 113 us  [fused_local(): pl.pallas_call(network_kernel, out_shape=low + [block(mels, samples), blo...]
where the time goes in v1:
time: 123 us; the launch traced here: 122 us
  Pallas kernels  122 us (99%)
    pallas_call x1, Pallas kernels, fused_local(): pl.pallas_call(network_kernel, out_shape=low + [block(mels, samples), blo...  113 us
    pallas_call x1, Pallas kernels, fused_local(): pl.pallas_call(finish_kernel, out_shape=large + [new_in[0], new_out[0]] +...  8.84 us

profile of v1, /device:TPU:0, one launch (start us, length us, event | category | flops | bytes accessed | tf_op | source)
XLA Modules:
  0.0 122.3 jit_solution(16612563457714000851)
XLA Ops:
  0.6 112.7 %network.1 = (bf16[2048,1024]{1,0:T(8,128)(2,1)}, bf16[2048,512]{1,0:T(8,128)(2,1)}, f32[80,2048]{1,0:T(8,128)}, f32[576,128]{1,0:T(8,128)}, f32[256,128]{1,0:T(8,128)}) custom-call(s32[256]{0:T(256)} %refs_0_.1, s32[1,4]{1,0:T(1,128)} %refs_1_.1, bf16[2048,512]{1,0:T(8,128)(2,1)} %bitcast.30, bf16[2048,512]{1,0:T(8,128)(2,1)} %bitcast.31, ...), custom_call_target="tpu_custom_call" | custom-call | tf_op jit(solution)/shard_map/network/pallas_call | solution.py:1121
  113.3 8.8 %finish.1 = (f32[2048,512]{1,0:T(8,128)}, f32[2048,512]{1,0:T(8,128)}, f32[2048,512]{1,0:T(8,128)}, f32[80,2048]{1,0:T(8,128)}, f32[552,128]{1,0:T(8,128)}, /*in...) custom-call(f32[576,128]{1,0:T(8,128)} %get-tuple-element.29.refs_0_, ...), custom_call_target="tpu_custom_call" | custom-call | tf_op jit(solution)/shard_map/finish/pallas_call | solution.py:1143

commit v2 on v1

--- a/solution.py
+++ b/solution.py
@@ -169,25 +169,27 @@
             self.to_x(1, 0, z, 1)
         self.to_sibling(0, z, half)
 
-    def z_copy(self, src, half, z):
-        return self.copy(self.at(0, src, half), self.z_sems.at[2 * src + half], self.p.z_peer(z))
-
-    def z_passed(self, n, half):
+    def z_copy(self, src, quarter, z):
+        part = self.count // 4
+        ref = self.stack.at[pl.ds(self.p.owner(0, src) * self.count + quarter * part, part)]
+        return self.copy(ref, self.z_sems.at[4 * src + quarter], self.p.z_peer(z))
+
+    def z_passed(self, n, quarter):
         p = self.p
         outer, inner = p.mirrored(0), p.mirrored(2)
         near, far, farthest = p.others
         src, z = ((p.z, inner), (near, inner), (far, outer), (farthest, outer))[n]
-        return self.z_copy(src, half, z)
-
-    def pass_on(self, n, half):
-        pl.when(self.p.near == 1)(lambda: self.z_passed(n, half).start())
+        return self.z_copy(src, quarter, z)
+
+    def pass_on(self, n, quarter):
+        pl.when(self.p.near == 1)(lambda: self.z_passed(n, quarter).start())
 
     def start(self):
         p = self.p
-        for half in range(2):
-            self.z_copy(p.z, half, p.mirrored(1 - p.near)).start()
-            self.sent += 1
-            self.pass_on(0, half)
+        for quarter in range(4):
+            self.z_copy(p.z, quarter, p.mirrored(1 - p.near)).start()
+            self.pass_on(0, quarter)
+        self.sent += 2
 
     def start_sides(self):
         for half in range(2):
@@ -195,8 +197,9 @@
 
     def relay(self, n, half):
         z = self.p.others[n]
-        self.arrived(self.at(0, z, half), self.z_sems.at[2 * z + half], self.p.z_peer(z))
-        self.pass_on(n + 1, half)
+        for quarter in (2 * half, 2 * half + 1):
+            self.z_copy(z, quarter, z).wait_recv()
+            self.pass_on(n + 1, quarter)
 
     def spread(self, n, half):
         self.sides(self.p.others[n], half)
@@ -245,7 +248,7 @@
             self.copy(self.bytes_of(8), self.s_sem.at[0], self.p.sibling).wait_send()
 
 
-GATHER_SEMS = [pltpu.SemaphoreType.DMA((n,)) for n in (1, 8, 12, 12, 1)]
+GATHER_SEMS = [pltpu.SemaphoreType.DMA((n,)) for n in (1, 16, 12, 12, 1)]
 
 
 def pick(which, zero, one):
@@ -776,8 +779,8 @@
         return [work.get(step, []) for step in REDUCE_ORDER]
 
 
-def loop(first, last, body):
-    lax.fori_loop(first, last, lambda t, _: (body(t), 0)[1], 0)
+def loop(first, last, body, unroll=1):
+    lax.fori_loop(first, last, lambda t, _: (body(t), 0)[1], 0, unroll=unroll)
 
 
 class Neighbours:
@@ -915,24 +918,28 @@
 
     n.make_masks()
     n.make_inverse()
-    for k, work in enumerate((make_rest, lambda: None, lambda: None)):
-        into.along_z(k)
-        work()
+    into.along_z(0)
+    into.along_z(1)
+    make_rest()
+    into.first(order[0])
+    into.along_z(2)
+    into.first(order[1])
+    for k in range(3):
         out.relay(k, 0)
         out.relay(k, 1)
-        into.first(order[k])
+    into.first(order[2])
     into.rest(order[0])
     into.first(order[3])
     near.start(*signal_halo)
-    out.start_sides()
-    for k in range(3):
-        out.spread(k, 0)
-        out.spread(k, 1)
     for copy in loads:
         copy.wait()
     n.make_delayed()
     for k in range(1, tiles):
         into.rest(order[k])
+    out.start_sides()
+    for k in range(3):
+        out.spread(k, 0)
+        out.spread(k, 1)
     into.finish()
     assemble_in(n.inverse, pairs_in, spread, n.full_in, 0)
     assemble_in(n.inverse, pairs_in, spread, n.full_in, 1)
@@ -954,13 +961,13 @@
     assemble_out(n.inverse, blocks_out, n.full_out, 1)
     n.state_one(tiles - 1)
     near.start(*state_halo)
-    loop(0, tiles - 1, n.state_one)
+    loop(0, tiles - 1, n.state_one, 3)
     for t in range(1, tiles):
         n.mend_delayed(t)
     near.arrived(*state_halo)
     n.mend_delayed(0)
 
-    loop(0, tiles, n.layer_two)
+    loop(0, tiles, n.layer_two, 2)
     n.units_two(0)
     near.start(*grad_halo)
     loop(1, tiles, n.units_two)
@@ -1000,9 +1007,9 @@
     run(*sum_out[6:8])
     n.weight_in(1, n.units2, 2)
     run(*sum_out[8:10])
-    loop(0, 2, n.layer_one_back)
+    loop(0, 2, n.layer_one_back, 2)
     run(sum_out[10])
-    loop(2, tiles, n.layer_one_back)
+    loop(2, tiles, n.layer_one_back, 2)
     run(*sum_out[11:13])
     n.weight_in(0, n.units1, 0)
     run(*sum_out[13:15])

time: 123 us -> 121 us (0.984)
  Pallas kernels: 122 us -> 120 us
    pallas_call x1, Pallas kernels: 113 us -> 111 us  [fused_local(): pl.pallas_call(network_kernel, out_shape=low + [block(mels, samples), blo...]
where the time goes in v2:
time: 121 us
  Pallas kernels  120 us (99%)
    pallas_call x1, Pallas kernels, fused_local(): pl.pallas_call(network_kernel, out_shape=low + [block(mels, samples), blo...  111 us
    pallas_call x1, Pallas kernels, fused_local(): pl.pallas_call(finish_kernel, out_shape=large + [new_in[0], new_out[0]] +...  8.84 us

profile of v2, /device:TPU:0, one launch (start us, length us, event | category | flops | bytes accessed | tf_op | source)
XLA Modules:
  0.0 121.1 jit_solution(6848596226138357929)
XLA Ops:
  0.6 111.4 %network.1 = (bf16[2048,1024]{1,0:T(8,128)(2,1)}, bf16[2048,512]{1,0:T(8,128)(2,1)}, f32[80,2048]{1,0:T(8,128)}, f32[576,128]{1,0:T(8,128)}, f32[256,128]{1,0:T(8,128)}) custom-call(s32[256]{0:T(256)} %refs_0_.1, s32[1,4]{1,0:T(1,128)} %refs_1_.1, bf16[2048,512]{1,0:T(8,128)(2,1)} %bitcast.30, bf16[2048,512]{1,0:T(8,128)(2,1)} %bitcast.31, ...), custom_call_target="tpu_custom_call" | custom-call | tf_op jit(solution)/shard_map/network/pallas_call | solution.py:1128
  112.1 8.8 %finish.1 = (f32[2048,512]{1,0:T(8,128)}, f32[2048,512]{1,0:T(8,128)}, f32[2048,512]{1,0:T(8,128)}, f32[80,2048]{1,0:T(8,128)}, f32[552,128]{1,0:T(8,128)}, /*in...) custom-call(f32[576,128]{1,0:T(8,128)} %get-tuple-element.29.refs_0_, ...), custom_call_target="tpu_custom_call" | custom-call | tf_op jit(solution)/shard_map/finish/pallas_call | solution.py:1150
